TPU v7x, 32 devices: a whole 2x2x4 slice. The times are simulated.
32 devices in a mesh: dp: 4 (over z), lat: 2 (over x), lon: 4 (over y, core).
Axes of the slice: x: 2, y: 2, z: 4, core: 2. Of those that a mesh axis runs over, the one named last changes fastest.
Arguments:
- initial_state: float32 [4, 128, 16, 512], P('dp', None, 'lat', 'lon'), may hold values from -6 to 6
- cotangent: float32 [4, 128, 16, 512], P('dp', None, 'lat', 'lon'), may hold values from -6 to 6
- diffusion: float32 [128], replicated, may hold values from 0.02 to 0.2
- norm_gain: float32 [128], replicated, may hold values from 0.5 to 1.5
- weight_in: bfloat16 [1024, 128], replicated, may hold values from -0.5 to 0.5
- bias_in: float32 [1024], replicated, may hold values from -3 to 3
- weight_out: bfloat16 [128, 1024], replicated, may hold values from -0.1875 to 0.1875
Outputs:
- final_state: float32 [4, 128, 16, 512], P('dp', None, 'lat', 'lon')
- state_grad: float32 [4, 128, 16, 512], P('dp', None, 'lat', 'lon')
- grad_in: float32 [1024, 128], replicated
- grad_out: float32 [128, 1024], replicated
All inputs are finite; a program needn't handle non-finite values.
Results may differ from a plain program's by a relative error of at most 0.006.
Values sent between devices are 32-bit elements; how exact they have to be, the bound alone decides.
A program may use at most 64 MiB of HBM per device.

v0:
```python
import math
import jax
import jax.numpy as jnp
from jax import lax
from jax.sharding import PartitionSpec as P

ROLL = 2
EPSILON = 1e-05
CONTRACT_LAST = (((1,), (1,)), ((), ()))
CONTRACT_FIRST = (((0,), (0,)), ((), ()))


def with_halo(block, sides, width, periodic):
    for axis, dim in sides:
        count = lax.axis_size(axis)
        forward = [(i, i + 1) for i in range(count - 1)]
        if periodic:
            forward.append((count - 1, 0))
        backward = [(target, source) for source, target in forward]
        low = lax.ppermute(
            lax.slice_in_dim(block, block.shape[dim] - width, None, axis=dim), axis, forward
        )
        high = lax.ppermute(lax.slice_in_dim(block, 0, width, axis=dim), axis, backward)
        block = jnp.concatenate([low, block, high], axis=dim)
    return block


def laplace(field):
    rows_ext = with_halo(field, (("lat", 1),), 1, False)
    cols_ext = with_halo(field, (("lon", 2),), 1, True)
    return (
        rows_ext[:, 2:, :]
        + rows_ext[:, :-2, :]
        + cols_ext[:, :, 2:]
        + cols_ext[:, :, :-2]
        - 4.0 * field
    )


def diffuse(field, diffusion):
    return field + diffusion[:, None, None] * laplace(field)


def physics(mixed, norm_gain, weight_in, bias_in, weight_out):
    inverse = lax.rsqrt(jnp.mean(mixed * mixed, axis=0) + EPSILON)
    normed = (mixed * inverse * norm_gain[:, None, None]).astype(jnp.bfloat16)
    flat_normed = normed.reshape(normed.shape[0], -1)
    pre_act = jnp.dot(weight_in, flat_normed, preferred_element_type=jnp.float32) + bias_in[:, None]
    squashed = jnp.tanh(pre_act)
    hidden = squashed.astype(jnp.bfloat16)
    update = jnp.dot(weight_out, hidden, preferred_element_type=jnp.float32)
    return (mixed + update.reshape(mixed.shape), (inverse, flat_normed, squashed, hidden))


def on_device(initial_state, cotangent, diffusion, norm_gain, weight_in, bias_in, weight_out):
    field = initial_state[0]
    channels = field.shape[0]
    saved_fields = []
    saved_mixed = []
    for section in range(ROLL):
        mixed = diffuse(field, diffusion)
        saved_fields.append(field)
        saved_mixed.append(mixed)
        field, unused = physics(mixed, norm_gain, weight_in, bias_in, weight_out)
    adjoint = cotangent[0]
    sum_in = jnp.zeros(weight_in.shape, jnp.float32)
    sum_out = jnp.zeros(weight_out.shape, jnp.float32)
    for section in reversed(range(ROLL)):
        mixed = diffuse(saved_fields[section], diffusion)
        unused, cache = physics(mixed, norm_gain, weight_in, bias_in, weight_out)
        inverse, flat_normed, squashed, hidden = cache
        adjoint_flat = adjoint.reshape(channels, -1).astype(jnp.bfloat16)
        term_out = lax.dot_general(
            adjoint_flat, hidden, CONTRACT_LAST, preferred_element_type=jnp.float32
        )
        hidden_adj = lax.dot_general(
            weight_out, adjoint_flat, CONTRACT_FIRST, preferred_element_type=jnp.float32
        )
        pre_adj = (hidden_adj * (1.0 - squashed * squashed)).astype(jnp.bfloat16)
        term_in = lax.dot_general(
            pre_adj, flat_normed, CONTRACT_LAST, preferred_element_type=jnp.float32
        )
        sum_in = sum_in + term_in
        sum_out = sum_out + term_out
        normed_adj = lax.dot_general(
            weight_in, pre_adj, CONTRACT_FIRST, preferred_element_type=jnp.float32
        )
        scaled_adj = normed_adj.reshape(mixed.shape) * norm_gain[:, None, None]
        inner = jnp.sum(scaled_adj * mixed, axis=0)
        mixed_adj = adjoint + inverse * scaled_adj - mixed * inverse**3 * inner / channels
        adjoint = mixed_adj + diffusion[:, None, None] * laplace(mixed_adj)
    sum_in, sum_out = lax.psum((sum_in, sum_out), ("dp", "lat", "lon"))
    columns_all = (
        lax.axis_size("dp")
        * lax.axis_size("lat")
        * lax.axis_size("lon")
        * field.shape[1]
        * field.shape[2]
    )
    factor = jnp.float32(1.0 / math.sqrt(columns_all))
    return (field[None], adjoint[None], sum_in * factor, sum_out * factor)


def solution(mesh):
    in_specs = (P("dp", None, "lat", "lon"), P("dp", None, "lat", "lon"), P(), P(), P(), P(), P())
    out_specs = (P("dp", None, "lat", "lon"), P("dp", None, "lat", "lon"), P(), P())
    return jax.shard_map(
        on_device, mesh=mesh, in_specs=in_specs, out_specs=out_specs, check_vma=False
    )
```

profile of v0, /device:TPU:0, one launch (start us, length us, event | category | flops | bytes accessed | tf_op | source)
XLA Modules:
  0.0 245.7 jit_solution(16050792861114076286)
XLA Ops:
  9.9 4.8 %collective-permute-start.1 = (f32[128,1,128]{2,1,0:T(1,128)S(1)}, f32[128,1,128]{2,1,0:T(1,128)S(1)}, u32[]{:S(2)}, u32[]{:S(2)}) collective-permute-start(f32[128,1,128]{2,1,0:T(1,128)S(1)} %get-tuple-element.31), channel_id=1, source_target_pairs={{0,4},{1,5},{2,6},{3,7},{8,12},{9,13},{10,14},{11,15},{16,20},{17,... | collective-permute-start | bytes 196616 | tf_op jit(solution)/shard_map/ppermute | solution.py:20
  16.2 1.6 collective-permute-start.2
  17.8 11.8 %collective-permute-done.2 = f32[128,8,1]{2,1,0:T(8,128)S(1)} collective-permute-done((f32[128,8,1]{2,1,0:T(8,128)S(1)}, f32[128,8,1]{2,1,0:T(8,128)S(1)}, u32[]{:S(2)}, u32[]{:S(2)}) %collective-permute-start.2) | collective-permute-done | bytes 4128 | tf_op jit(solution)/shard_map/ppermute | solution.py:23
  29.5 2.1 collective-permute-done.3
  31.7 2.6 %multiply_reduce_fusion.3 = (f32[8,128]{1,0:T(8,128)S(1)}, f32[128,8,128]{2,1,0:T(8,128)S(1)}) fusion(f32[128,8,128]{2,1,0:T(8,128)} %bitcast.68, f32[128,8,1]{2,1,0:T(8,128)S(1)} %collective-permute-done.3, f32[128,8,1]{2,1,0:T(8,128)S(1)} %collective-permute-done.2, f32[128,1,128]{2,1,0:T(1,128)S(1)} %collective-permute-done.1, ...), kind=kLoop, calls=%fused_computation.63 | loop fusion | flops 1702912 | bytes 1192448 | tf_op jit(solution)/shard_map/reduce_sum | solution.py:45
  36.0 2.0 copy-done.1
  40.4 4.5 %collective-permute-start.5 = (f32[128,1,128]{2,1,0:T(1,128)S(1)}, f32[128,1,128]{2,1,0:T(1,128)S(1)}, u32[]{:S(2)}, u32[]{:S(2)}) collective-permute-start(f32[128,1,128]{2,1,0:T(1,128)S(1)} %get-tuple-element.27), channel_id=1, source_target_pairs={{0,4},{1,5},{2,6},{3,7},{8,12},{9,13},{10,14},{11,15},{16,20},{17,... | collective-permute-start | bytes 196616 | tf_op jit(solution)/shard_map/ppermute | solution.py:20
  46.5 10.8 %collective-permute-done.6 = f32[128,8,1]{2,1,0:T(8,128)S(1)} collective-permute-done((f32[128,8,1]{2,1,0:T(8,128)S(1)}, f32[128,8,1]{2,1,0:T(8,128)S(1)}, u32[]{:S(2)}, u32[]{:S(2)}) %collective-permute-start.6) | collective-permute-done | bytes 4128 | tf_op jit(solution)/shard_map/ppermute | solution.py:23
  57.3 1.6 collective-permute-done.7
  61.2 2.0 copy-done.3
  65.0 3.2 %fusion = bf16[1024,1024]{0,1:T(8,128)(2,1)S(1)} fusion(f32[1024,1024]{1,0:T(8,128)} %copy-done.3, bf16[128,1024]{1,0:T(8,128)(2,1)S(1)} %copy-done, f32[1024]{0:T(1024)S(1)} %copy-done.13, bf16[16,8,8,128]{3,2,1,0:T(8,128)(2,1)} %bitcast.69), kind=kOutput, calls=%fused_computation.1 | convolution fusion | flops 273678336 | bytes 6819840 | tf_op jit(solution)/shard_map/dot_general | solution.py:76
  68.2 2.5 fusion.68
  70.7 2.0 copy.14
  74.0 2.3 fusion.36
  76.6 1.6 collective-permute-start.8
  78.2 4.5 %collective-permute-start.9 = (f32[128,1,128]{2,1,0:T(1,128)S(1)}, f32[128,1,128]{2,1,0:T(1,128)S(1)}, u32[]{:S(2)}, u32[]{:S(2)}) collective-permute-start(f32[128,1,128]{2,1,0:T(1,128)S(1)} %get-tuple-element.21), channel_id=1, source_target_pairs={{0,4},{1,5},{2,6},{3,7},{8,12},{9,13},{10,14},{11,15},{16,20},{17,... | collective-permute-start | bytes 196616 | tf_op jit(solution)/shard_map/ppermute | solution.py:20
  84.0 10.3 %collective-permute-done.10 = f32[128,8,1]{2,1,0:T(8,128)S(1)} collective-permute-done((f32[128,8,1]{2,1,0:T(8,128)S(1)}, f32[128,8,1]{2,1,0:T(8,128)S(1)}, u32[]{:S(2)}, u32[]{:S(2)}) %collective-permute-start.10) | collective-permute-done | bytes 4128 | tf_op jit(solution)/shard_map/ppermute | solution.py:23
  94.3 2.4 collective-permute-done.11
  100.6 1.6 fusion.3
  106.5 4.5 %collective-permute-start.13 = (f32[128,1,128]{2,1,0:T(1,128)S(1)}, f32[128,1,128]{2,1,0:T(1,128)S(1)}, u32[]{:S(2)}, u32[]{:S(2)}) collective-permute-start(f32[128,1,128]{2,1,0:T(1,128)S(1)} %get-tuple-element.17), channel_id=1, source_target_pairs={{0,4},{1,5},{2,6},{3,7},{8,12},{9,13},{10,14},{11,15},{16,20},{17,... | collective-permute-start | bytes 196616 | tf_op jit(solution)/shard_map/ppermute | solution.py:20
  111.9 12.9 %collective-permute-done.14 = f32[128,8,1]{2,1,0:T(8,128)S(1)} collective-permute-done((f32[128,8,1]{2,1,0:T(8,128)S(1)}, f32[128,8,1]{2,1,0:T(8,128)S(1)}, u32[]{:S(2)}, u32[]{:S(2)}) %collective-permute-start.14) | collective-permute-done | bytes 4128 | tf_op jit(solution)/shard_map/ppermute | solution.py:23
  124.8 1.6 collective-permute-done.15
  127.8 107.1 %all-reduce.3.cloned.1.call-done = (f32[1024,128]{1,0:T(8,128)}, f32[128,1024]{0,1:T(8,128)}) async-done(((f32[1024,128]{1,0:T(8,128)}, f32[128,1024]{0,1:T(8,128)}), (f32[1024,128]{1,0:T(8,128)}, f32[128,1024]{0,1:T(8,128)})) %all-reduce.3.cloned.1.call-update) | async-done | bytes 1048592 | tf_op jit(solution)/shard_map/psum | solution.py:92
  234.9 1.9 broadcast_multiply_fusion.1
  (84 shorter events, 28.9 us)
Async XLA Ops:
  7.2 30.8 %copy-start = (bf16[128,1024]{1,0:T(8,128)(2,1)S(1)}, bf16[128,1024]{1,0:T(8,128)(2,1)}, u32[]{:S(2)}) copy-start(bf16[128,1024]{1,0:T(8,128)(2,1)} %param.13) | copy-start | bytes 786436
  7.2 27.2 %copy-start.14 = (f32[128]{0:T(128)S(1)}, f32[128]{0:T(128)}, u32[]{:S(2)}) copy-start(f32[128]{0:T(128)} %param.10) | copy-start | bytes 1540
  7.2 28.1 %copy-start.5 = (bf16[1024,128]{1,0:T(8,128)(2,1)S(1)}, bf16[1024,128]{1,0:T(8,128)(2,1)}, u32[]{:S(2)}) copy-start(bf16[1024,128]{1,0:T(8,128)(2,1)} %param.11) | copy-start | bytes 786436
  7.2 227.7 %all-reduce.3.cloned.1.call-start = ((), (), s32[]{:S(2)}) async-start(), calls=%async_computation | async-start | bytes 2097152 | tf_op jit(solution)/shard_map/psum | solution.py:92
  8.6 23.1 %collective-permute-start = (f32[128,1,128]{2,1,0:T(1,128)S(1)}, f32[128,1,128]{2,1,0:T(1,128)S(1)}, u32[]{:S(2)}, u32[]{:S(2)}) collective-permute-start(f32[128,1,128]{2,1,0:T(1,128)S(1)} %get-tuple-element.30), channel_id=1, source_target_pairs={{4,0},{5,1},{6,2},{7,3},{12,8},{13,9},{14,10},{15,11},{20,16},{21,... | collective-permute-start | bytes 196616 | tf_op jit(solution)/shard_map/ppermute | solution.py:23
  9.9 21.8 %collective-permute-start.1 = (f32[128,1,128]{2,1,0:T(1,128)S(1)}, f32[128,1,128]{2,1,0:T(1,128)S(1)}, u32[]{:S(2)}, u32[]{:S(2)}) collective-permute-start(f32[128,1,128]{2,1,0:T(1,128)S(1)} %get-tuple-element.31), channel_id=1, source_target_pairs={{0,4},{1,5},{2,6},{3,7},{8,12},{9,13},{10,14},{11,15},{16,20},{17,... | collective-permute-start | bytes 196616 | tf_op jit(solution)/shard_map/ppermute | solution.py:20
  16.2 21.8 %copy-start.13 = (f32[1024]{0:T(1024)S(1)}, f32[1024]{0:T(1024)}, u32[]{:S(2)}) copy-start(f32[1024]{0:T(1024)} %param.12) | copy-start | bytes 12292
  16.2 13.4 %collective-permute-start.2 = (f32[128,8,1]{2,1,0:T(8,128)S(1)}, f32[128,8,1]{2,1,0:T(8,128)S(1)}, u32[]{:S(2)}, u32[]{:S(2)}) collective-permute-start(f32[128,8,1]{2,1,0:T(8,128)S(1)} %get-tuple-element.32), channel_id=1, source_target_pairs={{1,0},{2,1},{3,2},{0,3},{5,4},{6,5},{7,6},{4,7},{9,8},{10,9},{11,1... | collective-permute-start | bytes 12296 | tf_op jit(solution)/shard_map/ppermute | solution.py:23
  17.8 13.9 %collective-permute-start.3 = (f32[128,8,1]{2,1,0:T(8,128)S(1)}, f32[128,8,1]{2,1,0:T(8,128)S(1)}, u32[]{:S(2)}, u32[]{:S(2)}) collective-permute-start(f32[128,8,1]{2,1,0:T(8,128)S(1)} %get-tuple-element.33), channel_id=1, source_target_pairs={{0,1},{1,2},{2,3},{3,0},{4,5},{5,6},{6,7},{7,4},{8,9},{9,10},{10,1... | collective-permute-start | bytes 12296 | tf_op jit(solution)/shard_map/ppermute | solution.py:20
  38.0 20.9 %copy-start.15 = (f32[128]{0:T(128)S(1)}, f32[128]{0:T(128)}, u32[]{:S(2)}) copy-start(f32[128]{0:T(128)} %param.9) | copy-start | bytes 1540
  39.1 19.8 %collective-permute-start.4 = (f32[128,1,128]{2,1,0:T(1,128)S(1)}, f32[128,1,128]{2,1,0:T(1,128)S(1)}, u32[]{:S(2)}, u32[]{:S(2)}) collective-permute-start(f32[128,1,128]{2,1,0:T(1,128)S(1)} %get-tuple-element.26), channel_id=1, source_target_pairs={{4,0},{5,1},{6,2},{7,3},{12,8},{13,9},{14,10},{15,11},{20,16},{21,... | collective-permute-start | bytes 196616 | tf_op jit(solution)/shard_map/ppermute | solution.py:23
  40.4 18.5 %collective-permute-start.5 = (f32[128,1,128]{2,1,0:T(1,128)S(1)}, f32[128,1,128]{2,1,0:T(1,128)S(1)}, u32[]{:S(2)}, u32[]{:S(2)}) collective-permute-start(f32[128,1,128]{2,1,0:T(1,128)S(1)} %get-tuple-element.27), channel_id=1, source_target_pairs={{0,4},{1,5},{2,6},{3,7},{8,12},{9,13},{10,14},{11,15},{16,20},{17,... | collective-permute-start | bytes 196616 | tf_op jit(solution)/shard_map/ppermute | solution.py:20
  45.2 12.1 %collective-permute-start.6 = (f32[128,8,1]{2,1,0:T(8,128)S(1)}, f32[128,8,1]{2,1,0:T(8,128)S(1)}, u32[]{:S(2)}, u32[]{:S(2)}) collective-permute-start(f32[128,8,1]{2,1,0:T(8,128)S(1)} %get-tuple-element.28), channel_id=1, source_target_pairs={{1,0},{2,1},{3,2},{0,3},{5,4},{6,5},{7,6},{4,7},{9,8},{10,9},{11,1... | collective-permute-start | bytes 12296 | tf_op jit(solution)/shard_map/ppermute | solution.py:23
  45.3 13.7 %collective-permute-start.7 = (f32[128,8,1]{2,1,0:T(8,128)S(1)}, f32[128,8,1]{2,1,0:T(8,128)S(1)}, u32[]{:S(2)}, u32[]{:S(2)}) collective-permute-start(f32[128,8,1]{2,1,0:T(8,128)S(1)} %get-tuple-element.29), channel_id=1, source_target_pairs={{0,1},{1,2},{2,3},{3,0},{4,5},{5,6},{6,7},{7,4},{8,9},{9,10},{10,1... | collective-permute-start | bytes 12296 | tf_op jit(solution)/shard_map/ppermute | solution.py:20
  72.7 10.6 %copy-start.11 = (bf16[128,8,128]{2,1,0:T(8,128)(2,1)S(1)}, bf16[128,8,128]{2,1,0:T(8,128)(2,1)}, u32[]{:S(2)}) copy-start(bf16[128,8,128]{2,1,0:T(8,128)(2,1)} %copy-done.10) | copy-start | bytes 786436
  76.6 20.7 %copy-start.2 = (f32[1024,1024]{1,0:T(8,128)S(1)}, f32[1024,1024]{1,0:T(8,128)}, u32[]{:S(2)}) copy-start(f32[1024,1024]{1,0:T(8,128)} %copy-done.1) | copy-start | bytes 12582916
  76.6 20.1 %collective-permute-start.8 = (f32[128,1,128]{2,1,0:T(1,128)S(1)}, f32[128,1,128]{2,1,0:T(1,128)S(1)}, u32[]{:S(2)}, u32[]{:S(2)}) collective-permute-start(f32[128,1,128]{2,1,0:T(1,128)S(1)} %get-tuple-element.20), channel_id=1, source_target_pairs={{4,0},{5,1},{6,2},{7,3},{12,8},{13,9},{14,10},{15,11},{20,16},{21,... | collective-permute-start | bytes 196616 | tf_op jit(solution)/shard_map/ppermute | solution.py:23
  78.2 18.5 %collective-permute-start.9 = (f32[128,1,128]{2,1,0:T(1,128)S(1)}, f32[128,1,128]{2,1,0:T(1,128)S(1)}, u32[]{:S(2)}, u32[]{:S(2)}) collective-permute-start(f32[128,1,128]{2,1,0:T(1,128)S(1)} %get-tuple-element.21), channel_id=1, source_target_pairs={{0,4},{1,5},{2,6},{3,7},{8,12},{9,13},{10,14},{11,15},{16,20},{17,... | collective-permute-start | bytes 196616 | tf_op jit(solution)/shard_map/ppermute | solution.py:20
  82.7 11.6 %collective-permute-start.10 = (f32[128,8,1]{2,1,0:T(8,128)S(1)}, f32[128,8,1]{2,1,0:T(8,128)S(1)}, u32[]{:S(2)}, u32[]{:S(2)}) collective-permute-start(f32[128,8,1]{2,1,0:T(8,128)S(1)} %get-tuple-element.22), channel_id=1, source_target_pairs={{1,0},{2,1},{3,2},{0,3},{5,4},{6,5},{7,6},{4,7},{9,8},{10,9},{11,1... | collective-permute-start | bytes 12296 | tf_op jit(solution)/shard_map/ppermute | solution.py:23
  82.8 13.9 %collective-permute-start.11 = (f32[128,8,1]{2,1,0:T(8,128)S(1)}, f32[128,8,1]{2,1,0:T(8,128)S(1)}, u32[]{:S(2)}, u32[]{:S(2)}) collective-permute-start(f32[128,8,1]{2,1,0:T(8,128)S(1)} %get-tuple-element.23), channel_id=1, source_target_pairs={{0,1},{1,2},{2,3},{3,0},{4,5},{5,6},{6,7},{7,4},{8,9},{9,10},{10,1... | collective-permute-start | bytes 12296 | tf_op jit(solution)/shard_map/ppermute | solution.py:20
  105.2 21.2 %collective-permute-start.12 = (f32[128,1,128]{2,1,0:T(1,128)S(1)}, f32[128,1,128]{2,1,0:T(1,128)S(1)}, u32[]{:S(2)}, u32[]{:S(2)}) collective-permute-start(f32[128,1,128]{2,1,0:T(1,128)S(1)} %get-tuple-element.16), channel_id=1, source_target_pairs={{4,0},{5,1},{6,2},{7,3},{12,8},{13,9},{14,10},{15,11},{20,16},{21,... | collective-permute-start | bytes 196616 | tf_op jit(solution)/shard_map/ppermute | solution.py:23
  106.5 19.9 %collective-permute-start.13 = (f32[128,1,128]{2,1,0:T(1,128)S(1)}, f32[128,1,128]{2,1,0:T(1,128)S(1)}, u32[]{:S(2)}, u32[]{:S(2)}) collective-permute-start(f32[128,1,128]{2,1,0:T(1,128)S(1)} %get-tuple-element.17), channel_id=1, source_target_pairs={{0,4},{1,5},{2,6},{3,7},{8,12},{9,13},{10,14},{11,15},{16,20},{17,... | collective-permute-start | bytes 196616 | tf_op jit(solution)/shard_map/ppermute | solution.py:20
  111.3 13.5 %collective-permute-start.14 = (f32[128,8,1]{2,1,0:T(8,128)S(1)}, f32[128,8,1]{2,1,0:T(8,128)S(1)}, u32[]{:S(2)}, u32[]{:S(2)}) collective-permute-start(f32[128,8,1]{2,1,0:T(8,128)S(1)} %get-tuple-element.18), channel_id=1, source_target_pairs={{1,0},{2,1},{3,2},{0,3},{5,4},{6,5},{7,6},{4,7},{9,8},{10,9},{11,1... | collective-permute-start | bytes 12296 | tf_op jit(solution)/shard_map/ppermute | solution.py:23
  111.4 15.1 %collective-permute-start.15 = (f32[128,8,1]{2,1,0:T(8,128)S(1)}, f32[128,8,1]{2,1,0:T(8,128)S(1)}, u32[]{:S(2)}, u32[]{:S(2)}) collective-permute-start(f32[128,8,1]{2,1,0:T(8,128)S(1)} %get-tuple-element.19), channel_id=1, source_target_pairs={{0,1},{1,2},{2,3},{3,0},{4,5},{5,6},{6,7},{7,4},{8,9},{9,10},{10,1... | collective-permute-start | bytes 12296 | tf_op jit(solution)/shard_map/ppermute | solution.py:20
  (9 other events, 21.6 us)
Sparse Core Ops, SparseCore 0:
  105.1 129.8 all-reduce.2
where the time goes:
time: 246 us
  waiting for transfers between devices  161 us (65%)
  starting transfers between devices  27.2 us (11%)
  matrix products  15.2 us (6%)
  local copies, waits for them, and re-layouts  14.8 us (6%)
  between operations  14.4 us (6%)
  other arithmetic  13.5 us (5%)
    psum x1, waiting for transfers between devices, on_device(): sum_in, sum_out = lax.psum((sum_in, sum_out), ('dp', 'lat', 'lon'))  107 us
    ppermute x8, waiting for transfers between devices, with_halo(): lax.ppermute(lax.slice_in_dim(block, 0, width, axis=dim), axis, backward)  45.8 us
    ppermute x8, starting transfers between devices, with_halo(): lax.ppermute(lax.slice_in_dim(block, block.shape[dim] - width, None, axis...  20 us
    ppermute x8, waiting for transfers between devices, with_halo(): lax.ppermute(lax.slice_in_dim(block, block.shape[dim] - width, None, axis...  7.8 us
    unnamed x33, local copies, waits for them, and re-layouts  7.67 us
    ppermute x8, starting transfers between devices, with_halo(): lax.ppermute(lax.slice_in_dim(block, 0, width, axis=dim), axis, backward)  7.2 us
  transfers between devices with their start and end apart: 17, of which 9 were waited for; matrix products, arithmetic and copies ran while one was open for 2% of the time, Pallas kernels for 0%

commit v1 on v0

--- a/solution.py
+++ b/solution.py
@@ -8,6 +8,14 @@
 EPSILON = 1e-05
 CONTRACT_LAST = (((1,), (1,)), ((), ()))
 CONTRACT_FIRST = (((0,), (0,)), ((), ()))
+
+
+def rates_order(field_in):
+    across = "dp"
+    dev_axis = ("lat", "lon")
+    for to_i in (dev_axis, across):
+        field_in = lax.psum(field_in, to_i)
+    return field_in
 
 
 def with_halo(block, sides, width, periodic):
@@ -89,7 +97,7 @@
         inner = jnp.sum(scaled_adj * mixed, axis=0)
         mixed_adj = adjoint + inverse * scaled_adj - mixed * inverse**3 * inner / channels
         adjoint = mixed_adj + diffusion[:, None, None] * laplace(mixed_adj)
-    sum_in, sum_out = lax.psum((sum_in, sum_out), ("dp", "lat", "lon"))
+    sum_in, sum_out = rates_order((sum_in, sum_out))
     columns_all = (
         lax.axis_size("dp")
         * lax.axis_size("lat")

time: 246 us -> 226 us (0.919)
  waiting for transfers between devices: 161 us -> 137 us
    psum x1 -> x2, waiting for transfers between devices: 107 us -> 85 us  [rates_order(): field_in = lax.psum(field_in, to_i)]
  transfers between devices with their start and end apart: 17 -> 18, of which waited for: 9 -> 10; matrix products, arithmetic and copies ran while one was open for 2% -> 4% of each run, Pallas kernels for 0% -> 0%
where the time goes in v1:
time: 226 us
  waiting for transfers between devices  137 us (61%)
  starting transfers between devices  27.3 us (12%)
  matrix products  16 us (7%)
  local copies, waits for them, and re-layouts  15.8 us (7%)
  other arithmetic  15.4 us (7%)
  between operations  14.4 us (6%)
    psum x2, waiting for transfers between devices, rates_order(): field_in = lax.psum(field_in, to_i)  85 us
    ppermute x8, waiting for transfers between devices, with_halo(): lax.ppermute(lax.slice_in_dim(block, 0, width, axis=dim), axis, backward)  44.6 us
    ppermute x8, starting transfers between devices, with_halo(): lax.ppermute(lax.slice_in_dim(block, block.shape[dim] - width, None, axis...  20 us
    unnamed x33, local copies, waits for them, and re-layouts  7.64 us
    ppermute x8, starting transfers between devices, with_halo(): lax.ppermute(lax.slice_in_dim(block, 0, width, axis=dim), axis, backward)  7.2 us
    ppermute x8, waiting for transfers between devices, with_halo(): lax.ppermute(lax.slice_in_dim(block, block.shape[dim] - width, None, axis...  7.11 us
  transfers between devices with their start and end apart: 18, of which 10 were waited for; matrix products, arithmetic and copies ran while one was open for 4% of the time, Pallas kernels for 0%

profile of v1, /device:TPU:0, one launch (start us, length us, event | category | flops | bytes accessed | tf_op | source)
XLA Modules:
  0.0 225.7 jit_solution(11211050244715881305)
XLA Ops:
  9.9 4.8 %collective-permute-start.1 = (f32[128,1,128]{2,1,0:T(1,128)S(1)}, f32[128,1,128]{2,1,0:T(1,128)S(1)}, u32[]{:S(2)}, u32[]{:S(2)}) collective-permute-start(f32[128,1,128]{2,1,0:T(1,128)S(1)} %get-tuple-element.33), channel_id=1, source_target_pairs={{0,4},{1,5},{2,6},{3,7},{8,12},{9,13},{10,14},{11,15},{16,20},{17,... | collective-permute-start | bytes 196616 | tf_op jit(solution)/shard_map/ppermute | solution.py:28
  16.2 1.6 collective-permute-start.2
  17.8 11.8 %collective-permute-done.2 = f32[128,8,1]{2,1,0:T(8,128)S(1)} collective-permute-done((f32[128,8,1]{2,1,0:T(8,128)S(1)}, f32[128,8,1]{2,1,0:T(8,128)S(1)}, u32[]{:S(2)}, u32[]{:S(2)}) %collective-permute-start.2) | collective-permute-done | bytes 4128 | tf_op jit(solution)/shard_map/ppermute | solution.py:31
  29.6 2.1 collective-permute-done.3
  31.7 2.7 %multiply_reduce_fusion.3 = (f32[8,128]{1,0:T(8,128)S(1)}, f32[128,8,128]{2,1,0:T(8,128)S(1)}) fusion(f32[128,8,128]{2,1,0:T(8,128)} %bitcast.68, f32[128,8,1]{2,1,0:T(8,128)S(1)} %collective-permute-done.3, f32[128,8,1]{2,1,0:T(8,128)S(1)} %collective-permute-done.2, f32[128,1,128]{2,1,0:T(1,128)S(1)} %collective-permute-done.1, ...), kind=kLoop, calls=%fused_computation.63 | loop fusion | flops 1702912 | bytes 1192448 | tf_op jit(solution)/shard_map/reduce_sum | solution.py:53
  36.2 2.0 copy-done.1
  40.6 4.5 %collective-permute-start.5 = (f32[128,1,128]{2,1,0:T(1,128)S(1)}, f32[128,1,128]{2,1,0:T(1,128)S(1)}, u32[]{:S(2)}, u32[]{:S(2)}) collective-permute-start(f32[128,1,128]{2,1,0:T(1,128)S(1)} %get-tuple-element.29), channel_id=1, source_target_pairs={{0,4},{1,5},{2,6},{3,7},{8,12},{9,13},{10,14},{11,15},{16,20},{17,... | collective-permute-start | bytes 196616 | tf_op jit(solution)/shard_map/ppermute | solution.py:28
  46.6 10.8 %collective-permute-done.6 = f32[128,8,1]{2,1,0:T(8,128)S(1)} collective-permute-done((f32[128,8,1]{2,1,0:T(8,128)S(1)}, f32[128,8,1]{2,1,0:T(8,128)S(1)}, u32[]{:S(2)}, u32[]{:S(2)}) %collective-permute-start.6) | collective-permute-done | bytes 4128 | tf_op jit(solution)/shard_map/ppermute | solution.py:31
  57.4 1.7 collective-permute-done.7
  61.4 2.0 copy-done.3
  65.1 3.2 %fusion = bf16[1024,1024]{0,1:T(8,128)(2,1)S(1)} fusion(f32[1024,1024]{1,0:T(8,128)} %copy-done.3, bf16[128,1024]{1,0:T(8,128)(2,1)S(1)} %copy-done, f32[1024]{0:T(1024)S(1)} %copy-done.13, bf16[16,8,8,128]{3,2,1,0:T(8,128)(2,1)} %bitcast.69), kind=kOutput, calls=%fused_computation.1 | convolution fusion | flops 273678336 | bytes 6819840 | tf_op jit(solution)/shard_map/dot_general | solution.py:84
  68.4 2.5 %fusion.68 = f32[1024,128]{1,0:T(8,128)} fusion(bf16[1024,1024]{0,1:T(8,128)(2,1)S(1)} %fusion, bf16[1024,128]{1,0:T(8,128)(2,1)} %param.11), kind=kOutput, calls=%fused_computation.98 | convolution fusion | flops 268435456 | bytes 2883584 | tf_op jit(solution)/shard_map/dot_general | solution.py:93
  70.8 2.0 copy.14
  74.1 2.3 %fusion.36 = (f32[128,8,128]{2,1,0:T(8,128)S(1)}, f32[1,128,8,128]{3,2,1,0:T(8,128)}) fusion(f32[1,128,8,128]{3,2,1,0:T(8,128)} %param.8, f32[128,8,128]{2,1,0:T(8,128)S(1)} %get-tuple-element.15, f32[128,8,128]{2,1,0:T(8,128)} %copy.14, f32[8,128]{1,0:T(8,128)S(1)} %multiply_reduce_fusion.1, f32[8,128]{1,0:T(8,128)S(1)} %get-tuple-element.38, ...), kind=kLoop, calls=%fused_computation.55 | loop fusion | flops 1048576 | bytes 3158528 | tf_op jit(solution)/shard_map/sub | solution.py:98
  76.7 1.6 collective-permute-start.8
  78.3 4.5 %collective-permute-start.9 = (f32[128,1,128]{2,1,0:T(1,128)S(1)}, f32[128,1,128]{2,1,0:T(1,128)S(1)}, u32[]{:S(2)}, u32[]{:S(2)}) collective-permute-start(f32[128,1,128]{2,1,0:T(1,128)S(1)} %get-tuple-element.23), channel_id=1, source_target_pairs={{0,4},{1,5},{2,6},{3,7},{8,12},{9,13},{10,14},{11,15},{16,20},{17,... | collective-permute-start | bytes 196616 | tf_op jit(solution)/shard_map/ppermute | solution.py:28
  84.2 10.3 %collective-permute-done.10 = f32[128,8,1]{2,1,0:T(8,128)S(1)} collective-permute-done((f32[128,8,1]{2,1,0:T(8,128)S(1)}, f32[128,8,1]{2,1,0:T(8,128)S(1)}, u32[]{:S(2)}, u32[]{:S(2)}) %collective-permute-start.10) | collective-permute-done | bytes 4128 | tf_op jit(solution)/shard_map/ppermute | solution.py:31
  94.5 2.3 %collective-permute-done.11 = f32[128,8,1]{2,1,0:T(8,128)S(1)} collective-permute-done((f32[128,8,1]{2,1,0:T(8,128)S(1)}, f32[128,8,1]{2,1,0:T(8,128)S(1)}, u32[]{:S(2)}, u32[]{:S(2)}) %collective-permute-start.11) | collective-permute-done | bytes 4128 | tf_op jit(solution)/shard_map/ppermute | solution.py:28
  101.4 1.6 fusion.3
  107.5 53.7 %all-reduce.5.cloned.1.call-done = (f32[1024,128]{1,0:T(8,128)}, f32[128,1024]{0,1:T(8,128)}) async-done(((f32[1024,128]{1,0:T(8,128)}, f32[128,1024]{0,1:T(8,128)}), (f32[1024,128]{1,0:T(8,128)}, f32[128,1024]{0,1:T(8,128)})) %all-reduce.5.cloned.1.call-update) | async-done | bytes 1048592 | tf_op jit(solution)/shard_map/psum | solution.py:17
  164.1 4.5 %collective-permute-start.13 = (f32[128,1,128]{2,1,0:T(1,128)S(1)}, f32[128,1,128]{2,1,0:T(1,128)S(1)}, u32[]{:S(2)}, u32[]{:S(2)}) collective-permute-start(f32[128,1,128]{2,1,0:T(1,128)S(1)} %get-tuple-element.19), channel_id=1, source_target_pairs={{0,4},{1,5},{2,6},{3,7},{8,12},{9,13},{10,14},{11,15},{16,20},{17,... | collective-permute-start | bytes 196616 | tf_op jit(solution)/shard_map/ppermute | solution.py:28
  169.4 11.8 %collective-permute-done.14 = f32[128,8,1]{2,1,0:T(8,128)S(1)} collective-permute-done((f32[128,8,1]{2,1,0:T(8,128)S(1)}, f32[128,8,1]{2,1,0:T(8,128)S(1)}, u32[]{:S(2)}, u32[]{:S(2)}) %collective-permute-start.14) | collective-permute-done | bytes 4128 | tf_op jit(solution)/shard_map/ppermute | solution.py:31
  183.6 31.3 %all-reduce.7.cloned.1.call-done = (f32[1024,128]{1,0:T(8,128)}, f32[128,1024]{0,1:T(8,128)}) async-done(((f32[1024,128]{1,0:T(8,128)}, f32[128,1024]{0,1:T(8,128)}), (f32[1024,128]{1,0:T(8,128)}, f32[128,1024]{0,1:T(8,128)})) %all-reduce.7.cloned.1.call-update) | async-done | bytes 1048592 | tf_op jit(solution)/shard_map/psum | solution.py:17
  214.9 1.9 broadcast_multiply_fusion.1
  (87 shorter events, 33.6 us)
Async XLA Ops:
  7.2 31.0 %copy-start = (bf16[128,1024]{1,0:T(8,128)(2,1)S(1)}, bf16[128,1024]{1,0:T(8,128)(2,1)}, u32[]{:S(2)}) copy-start(bf16[128,1024]{1,0:T(8,128)(2,1)} %param.13) | copy-start | bytes 786436
  7.2 27.3 %copy-start.14 = (f32[128]{0:T(128)S(1)}, f32[128]{0:T(128)}, u32[]{:S(2)}) copy-start(f32[128]{0:T(128)} %param.10) | copy-start | bytes 1540
  7.2 28.2 %copy-start.5 = (bf16[1024,128]{1,0:T(8,128)(2,1)S(1)}, bf16[1024,128]{1,0:T(8,128)(2,1)}, u32[]{:S(2)}) copy-start(bf16[1024,128]{1,0:T(8,128)(2,1)} %param.11) | copy-start | bytes 786436
  7.2 154.0 %all-reduce.5.cloned.1.call-start = ((), (), s32[]{:S(2)}) async-start(), calls=%async_computation | async-start | bytes 2097152 | tf_op jit(solution)/shard_map/psum | solution.py:17
  8.6 23.1 %collective-permute-start = (f32[128,1,128]{2,1,0:T(1,128)S(1)}, f32[128,1,128]{2,1,0:T(1,128)S(1)}, u32[]{:S(2)}, u32[]{:S(2)}) collective-permute-start(f32[128,1,128]{2,1,0:T(1,128)S(1)} %get-tuple-element.32), channel_id=1, source_target_pairs={{4,0},{5,1},{6,2},{7,3},{12,8},{13,9},{14,10},{15,11},{20,16},{21,... | collective-permute-start | bytes 196616 | tf_op jit(solution)/shard_map/ppermute | solution.py:31
  9.9 21.8 %collective-permute-start.1 = (f32[128,1,128]{2,1,0:T(1,128)S(1)}, f32[128,1,128]{2,1,0:T(1,128)S(1)}, u32[]{:S(2)}, u32[]{:S(2)}) collective-permute-start(f32[128,1,128]{2,1,0:T(1,128)S(1)} %get-tuple-element.33), channel_id=1, source_target_pairs={{0,4},{1,5},{2,6},{3,7},{8,12},{9,13},{10,14},{11,15},{16,20},{17,... | collective-permute-start | bytes 196616 | tf_op jit(solution)/shard_map/ppermute | solution.py:28
  16.2 21.9 %copy-start.13 = (f32[1024]{0:T(1024)S(1)}, f32[1024]{0:T(1024)}, u32[]{:S(2)}) copy-start(f32[1024]{0:T(1024)} %param.12) | copy-start | bytes 12292
  16.2 13.4 %collective-permute-start.2 = (f32[128,8,1]{2,1,0:T(8,128)S(1)}, f32[128,8,1]{2,1,0:T(8,128)S(1)}, u32[]{:S(2)}, u32[]{:S(2)}) collective-permute-start(f32[128,8,1]{2,1,0:T(8,128)S(1)} %get-tuple-element.34), channel_id=1, source_target_pairs={{1,0},{2,1},{3,2},{0,3},{5,4},{6,5},{7,6},{4,7},{9,8},{10,9},{11,1... | collective-permute-start | bytes 12296 | tf_op jit(solution)/shard_map/ppermute | solution.py:31
  17.8 13.9 %collective-permute-start.3 = (f32[128,8,1]{2,1,0:T(8,128)S(1)}, f32[128,8,1]{2,1,0:T(8,128)S(1)}, u32[]{:S(2)}, u32[]{:S(2)}) collective-permute-start(f32[128,8,1]{2,1,0:T(8,128)S(1)} %get-tuple-element.35), channel_id=1, source_target_pairs={{0,1},{1,2},{2,3},{3,0},{4,5},{5,6},{6,7},{7,4},{8,9},{9,10},{10,1... | collective-permute-start | bytes 12296 | tf_op jit(solution)/shard_map/ppermute | solution.py:28
  38.1 20.9 %copy-start.15 = (f32[128]{0:T(128)S(1)}, f32[128]{0:T(128)}, u32[]{:S(2)}) copy-start(f32[128]{0:T(128)} %param.9) | copy-start | bytes 1540
  39.3 19.8 %collective-permute-start.4 = (f32[128,1,128]{2,1,0:T(1,128)S(1)}, f32[128,1,128]{2,1,0:T(1,128)S(1)}, u32[]{:S(2)}, u32[]{:S(2)}) collective-permute-start(f32[128,1,128]{2,1,0:T(1,128)S(1)} %get-tuple-element.28), channel_id=1, source_target_pairs={{4,0},{5,1},{6,2},{7,3},{12,8},{13,9},{14,10},{15,11},{20,16},{21,... | collective-permute-start | bytes 196616 | tf_op jit(solution)/shard_map/ppermute | solution.py:31
  40.6 18.5 %collective-permute-start.5 = (f32[128,1,128]{2,1,0:T(1,128)S(1)}, f32[128,1,128]{2,1,0:T(1,128)S(1)}, u32[]{:S(2)}, u32[]{:S(2)}) collective-permute-start(f32[128,1,128]{2,1,0:T(1,128)S(1)} %get-tuple-element.29), channel_id=1, source_target_pairs={{0,4},{1,5},{2,6},{3,7},{8,12},{9,13},{10,14},{11,15},{16,20},{17,... | collective-permute-start | bytes 196616 | tf_op jit(solution)/shard_map/ppermute | solution.py:28
  45.3 12.1 %collective-permute-start.6 = (f32[128,8,1]{2,1,0:T(8,128)S(1)}, f32[128,8,1]{2,1,0:T(8,128)S(1)}, u32[]{:S(2)}, u32[]{:S(2)}) collective-permute-start(f32[128,8,1]{2,1,0:T(8,128)S(1)} %get-tuple-element.30), channel_id=1, source_target_pairs={{1,0},{2,1},{3,2},{0,3},{5,4},{6,5},{7,6},{4,7},{9,8},{10,9},{11,1... | collective-permute-start | bytes 12296 | tf_op jit(solution)/shard_map/ppermute | solution.py:31
  45.4 13.7 %collective-permute-start.7 = (f32[128,8,1]{2,1,0:T(8,128)S(1)}, f32[128,8,1]{2,1,0:T(8,128)S(1)}, u32[]{:S(2)}, u32[]{:S(2)}) collective-permute-start(f32[128,8,1]{2,1,0:T(8,128)S(1)} %get-tuple-element.31), channel_id=1, source_target_pairs={{0,1},{1,2},{2,3},{3,0},{4,5},{5,6},{6,7},{7,4},{8,9},{9,10},{10,1... | collective-permute-start | bytes 12296 | tf_op jit(solution)/shard_map/ppermute | solution.py:28
  76.7 21.5 %copy-start.2 = (f32[1024,1024]{1,0:T(8,128)S(1)}, f32[1024,1024]{1,0:T(8,128)}, u32[]{:S(2)}) copy-start(f32[1024,1024]{1,0:T(8,128)} %copy-done.1) | copy-start | bytes 12582916
  76.7 20.1 %collective-permute-start.8 = (f32[128,1,128]{2,1,0:T(1,128)S(1)}, f32[128,1,128]{2,1,0:T(1,128)S(1)}, u32[]{:S(2)}, u32[]{:S(2)}) collective-permute-start(f32[128,1,128]{2,1,0:T(1,128)S(1)} %get-tuple-element.22), channel_id=1, source_target_pairs={{4,0},{5,1},{6,2},{7,3},{12,8},{13,9},{14,10},{15,11},{20,16},{21,... | collective-permute-start | bytes 196616 | tf_op jit(solution)/shard_map/ppermute | solution.py:31
  78.3 18.5 %collective-permute-start.9 = (f32[128,1,128]{2,1,0:T(1,128)S(1)}, f32[128,1,128]{2,1,0:T(1,128)S(1)}, u32[]{:S(2)}, u32[]{:S(2)}) collective-permute-start(f32[128,1,128]{2,1,0:T(1,128)S(1)} %get-tuple-element.23), channel_id=1, source_target_pairs={{0,4},{1,5},{2,6},{3,7},{8,12},{9,13},{10,14},{11,15},{16,20},{17,... | collective-permute-start | bytes 196616 | tf_op jit(solution)/shard_map/ppermute | solution.py:28
  82.8 11.6 %collective-permute-start.10 = (f32[128,8,1]{2,1,0:T(8,128)S(1)}, f32[128,8,1]{2,1,0:T(8,128)S(1)}, u32[]{:S(2)}, u32[]{:S(2)}) collective-permute-start(f32[128,8,1]{2,1,0:T(8,128)S(1)} %get-tuple-element.24), channel_id=1, source_target_pairs={{1,0},{2,1},{3,2},{0,3},{5,4},{6,5},{7,6},{4,7},{9,8},{10,9},{11,1... | collective-permute-start | bytes 12296 | tf_op jit(solution)/shard_map/ppermute | solution.py:31
  82.9 13.9 %collective-permute-start.11 = (f32[128,8,1]{2,1,0:T(8,128)S(1)}, f32[128,8,1]{2,1,0:T(8,128)S(1)}, u32[]{:S(2)}, u32[]{:S(2)}) collective-permute-start(f32[128,8,1]{2,1,0:T(8,128)S(1)} %get-tuple-element.25), channel_id=1, source_target_pairs={{0,1},{1,2},{2,3},{3,0},{4,5},{5,6},{6,7},{7,4},{8,9},{9,10},{10,1... | collective-permute-start | bytes 12296 | tf_op jit(solution)/shard_map/ppermute | solution.py:28
  104.7 110.2 %all-reduce.7.cloned.1.call-start = ((), (), s32[]{:S(2)}) async-start(), calls=%async_computation.1 | async-start | bytes 2097152 | tf_op jit(solution)/shard_map/psum | solution.py:17
  162.8 19.4 %collective-permute-start.12 = (f32[128,1,128]{2,1,0:T(1,128)S(1)}, f32[128,1,128]{2,1,0:T(1,128)S(1)}, u32[]{:S(2)}, u32[]{:S(2)}) collective-permute-start(f32[128,1,128]{2,1,0:T(1,128)S(1)} %get-tuple-element.18), channel_id=1, source_target_pairs={{4,0},{5,1},{6,2},{7,3},{12,8},{13,9},{14,10},{15,11},{20,16},{21,... | collective-permute-start | bytes 196616 | tf_op jit(solution)/shard_map/ppermute | solution.py:31
  164.1 18.1 %collective-permute-start.13 = (f32[128,1,128]{2,1,0:T(1,128)S(1)}, f32[128,1,128]{2,1,0:T(1,128)S(1)}, u32[]{:S(2)}, u32[]{:S(2)}) collective-permute-start(f32[128,1,128]{2,1,0:T(1,128)S(1)} %get-tuple-element.19), channel_id=1, source_target_pairs={{0,4},{1,5},{2,6},{3,7},{8,12},{9,13},{10,14},{11,15},{16,20},{17,... | collective-permute-start | bytes 196616 | tf_op jit(solution)/shard_map/ppermute | solution.py:28
  168.9 12.4 %collective-permute-start.14 = (f32[128,8,1]{2,1,0:T(8,128)S(1)}, f32[128,8,1]{2,1,0:T(8,128)S(1)}, u32[]{:S(2)}, u32[]{:S(2)}) collective-permute-start(f32[128,8,1]{2,1,0:T(8,128)S(1)} %get-tuple-element.20), channel_id=1, source_target_pairs={{1,0},{2,1},{3,2},{0,3},{5,4},{6,5},{7,6},{4,7},{9,8},{10,9},{11,1... | collective-permute-start | bytes 12296 | tf_op jit(solution)/shard_map/ppermute | solution.py:31
  168.9 13.3 %collective-permute-start.15 = (f32[128,8,1]{2,1,0:T(8,128)S(1)}, f32[128,8,1]{2,1,0:T(8,128)S(1)}, u32[]{:S(2)}, u32[]{:S(2)}) collective-permute-start(f32[128,8,1]{2,1,0:T(8,128)S(1)} %get-tuple-element.21), channel_id=1, source_target_pairs={{0,1},{1,2},{2,3},{3,0},{4,5},{5,6},{6,7},{7,4},{8,9},{9,10},{10,1... | collective-permute-start | bytes 12296 | tf_op jit(solution)/shard_map/ppermute | solution.py:28
  (10 other events, 31.4 us)
Sparse Core Ops, SparseCore 0:
  104.8 56.3 all-reduce.4
  163.6 51.2 all-reduce.6
